TPU v7x, 32 devices: a whole 2x2x4 slice. The times are simulated.
32 devices in a mesh: groups: 2 (over y), trade: 4 (over z), date: 2 (over x), scen: 2 (over core).
Axes of the slice: x: 2, y: 2, z: 4, core: 2. Of those that a mesh axis runs over, the one named last changes fastest.
Arguments:
- cash_flows: bfloat16 [1024, 64], P('trade'), may hold values from -0.8984375 to 0.8984375
- coupon_dates: int32 [1024, 64], P('trade'), may hold values from 0 to 127, as said below
- trade_sets: int32 [1024], P('trade'), may hold values from 0 to 511, as said below
- set_slots: int32 [512], replicated, may hold values from 0 to 511, as said below
- set_lags: int32 [512], P('trade'), may hold values from 0 to 4
- thresholds: float32 [512], P('trade'), may hold values from 0.05 to 1
- set_cpty: int32 [512], P('trade'), may hold values from 0 to 127
- discounts: bfloat16 [128, 128, 512], P('date', None, ('groups', 'scen')), parts along dimension 2, may hold values from 0.29882812 to 1
- default_probs: float32 [128, 128], P(None, 'date'), may hold values from 0.004 to 0.04
- loss_given: float32 [128], replicated, may hold values from 0.4 to 0.9
- cva_cotangent: float32 [128], replicated, may hold values from -6 to 6
Outputs:
- credit_charge: float32 [256], P('groups'), parts along dimension 0
- flow_grads: float32 [2048, 64], P(('groups', 'trade')), parts along dimension 0
There are 2 independent parts, one for each index of `groups`. A program takes and returns all parts, laid end to end along the dimension named above; an argument that names none is the same for every part. Nothing has to cross between parts.
Inputs may be any that keep to these rules, and one draw needn't show every extreme that they name: `coupon_dates`: the 64 dates of one swap are distinct. Call set_slots[trade_sets[n]] // 128 the owner of swap n; among the 256 swaps of one device at most 128 have the same owner, and some owner has exactly 128 swaps of every device. `set_slots`: each position is taken by exactly one netting set.
All inputs are finite; a program needn't handle non-finite values.
Results may differ from a plain program's by a relative error of at most 0.0027.
Values may be sent and summed in bfloat16 or wider, within the bound.
A program may use at most 128 MiB of HBM per device.

v0:
```python
import jax
import jax.numpy as jnp
from jax import lax
from jax.sharding import PartitionSpec as P

LAGMAX = 4


SMOOTH = 0.1


def from_behind(block, axis, distance):
    devices = range(lax.axis_size(axis))
    route = [(i - distance, i) for i in devices if i - distance in devices]
    return lax.ppermute(block, axis, route)


def for_sending(x):
    return jax.tree.map(lambda a: a.astype(jnp.bfloat16) if a.dtype == jnp.float32 else a, x)


def coupon_grid(cash_flows, coupon_dates, date_count):
    trade_count = cash_flows.shape[0]
    block_width = min(128, trade_count)
    date_axis = jnp.arange(date_count, dtype=jnp.int32)

    def per_block(inputs):
        amounts, moments = inputs
        matched = moments[:, :, None] == date_axis[None, None, :]
        return jnp.sum(
            jnp.where(matched, amounts.astype(jnp.float32)[:, :, None], jnp.float32(0.0)), axis=1
        )

    blocks = (
        cash_flows.reshape(trade_count // block_width, block_width, -1),
        coupon_dates.reshape(trade_count // block_width, block_width, -1),
    )
    return lax.map(per_block, blocks).reshape(trade_count, date_count)


def route_trades(trade_sets, set_slots, rows_dev, owner_count, capacity):
    positions = jnp.take(set_slots, trade_sets)
    owners = positions // rows_dev
    local_rows = positions - owners * rows_dev
    owner_axis = jnp.arange(owner_count, dtype=jnp.int32)
    picked = (owners[:, None] == owner_axis[None, :]).astype(jnp.int32)
    before = jnp.cumsum(picked, axis=0) - picked
    slot_ranks = jnp.sum(before * picked, axis=1)
    return (positions, local_rows, owners * capacity + slot_ranks)


def per_device(
    cash_flows,
    coupon_dates,
    trade_sets,
    set_slots,
    set_lags,
    thresholds,
    set_cpty,
    discounts,
    default_probs,
    loss_given,
    cva_cotangent,
):
    rows_dev = set_lags.shape[0]
    owner_count = lax.axis_size("trade")
    trade_count = cash_flows.shape[0]
    capacity = 2 * trade_count // owner_count
    span_dev = discounts.shape[0]
    date_count = discounts.shape[1]
    market_paths = discounts.shape[2] * lax.axis_size("scen")
    counterparties = loss_given.shape[0]
    positions, local_rows, slots_used = route_trades(
        trade_sets, set_slots, rows_dev, owner_count, capacity
    )
    trade_flows = coupon_grid(cash_flows, coupon_dates, date_count).astype(jnp.bfloat16)
    member = (
        positions[None, :]
        == jnp.arange(rows_dev * lax.axis_size("trade"), dtype=jnp.int32)[:, None]
    ).astype(jnp.bfloat16)
    set_flows = lax.psum_scatter(
        jnp.dot(member, trade_flows, preferred_element_type=jnp.float32),
        "trade",
        scatter_dimension=0,
        tiled=True,
    )
    set_flows = set_flows.astype(jnp.bfloat16)
    first_date = lax.axis_index("date") * span_dev
    own_dates = first_date + jnp.arange(span_dev, dtype=jnp.int32)
    date_axis = jnp.arange(date_count, dtype=jnp.int32)
    forward = jnp.where(
        date_axis[None, :, None] > own_dates[:, None, None], discounts, jnp.zeros((), jnp.bfloat16)
    )
    lag_rows = set_lags[:, None, None]
    values = jnp.einsum("pu,tus->pts", set_flows, forward, preferred_element_type=jnp.float32)
    earlier = from_behind(values[:, span_dev - LAGMAX :].astype(jnp.bfloat16), "date", 1).astype(
        jnp.float32
    )
    padded = jnp.concatenate([earlier, values], axis=1)
    lagged = jnp.zeros_like(values)
    for offset in range(LAGMAX + 1):
        lagged = jnp.where(
            lag_rows == offset, padded[:, LAGMAX - offset : LAGMAX - offset + span_dev], lagged
        )
    in_range = (own_dates[None, :] >= set_lags[:, None])[:, :, None]
    over_limit = (lagged - thresholds[:, None, None]) / SMOOTH
    collateral = jnp.where(in_range, SMOOTH * jax.nn.softplus(over_limit), jnp.float32(0.0))
    margin_gap = values - collateral
    exposure = SMOOTH * jax.nn.softplus(margin_gap / SMOOTH)
    exposure_curve = jnp.sum(exposure, axis=2)
    member_sets = (
        set_cpty[:, None] == jnp.arange(counterparties, dtype=jnp.int32)[None, :]
    ).astype(jnp.float32)
    hazard_intensity = jnp.dot(member_sets, default_probs, precision=lax.Precision.HIGHEST)
    notional_scale_factors = jnp.dot(
        member_sets,
        jnp.stack([loss_given, loss_given * cva_cotangent], axis=1),
        precision=lax.Precision.HIGHEST,
    )
    netting_set_contributions = (
        jnp.sum(hazard_intensity * exposure_curve, axis=1)
        * notional_scale_factors[:, 0]
        / market_paths
    )
    partial_charge = jnp.dot(
        netting_set_contributions, member_sets, precision=lax.Precision.HIGHEST
    )
    credit_charge = lax.psum(partial_charge, ("trade", "date", "scen"))
    netting_set_gather = hazard_intensity * (notional_scale_factors[:, 1] / market_paths)[:, None]
    direct = netting_set_gather[:, :, None] * jax.nn.sigmoid(margin_gap / SMOOTH)
    backward = jnp.where(in_range, -direct * jax.nn.sigmoid(over_limit), jnp.float32(0.0))
    carried = jnp.zeros_like(padded)
    for offset in range(LAGMAX + 1):
        picked = jnp.where(lag_rows == offset, backward, jnp.float32(0.0))
        carried = carried + jnp.pad(picked, ((0, 0), (LAGMAX - offset, offset), (0, 0)))
    returned = from_behind(for_sending(carried[:, :LAGMAX]), "date", -1)
    value_grads = (
        direct + carried[:, LAGMAX:] + jnp.pad(returned, ((0, 0), (span_dev - LAGMAX, 0), (0, 0)))
    )
    value_grads = value_grads.astype(jnp.bfloat16)
    partial_grads = jnp.einsum(
        "pts,tus->pu", value_grads, forward, preferred_element_type=jnp.float32
    )
    set_grads = lax.psum(partial_grads, ("date", "scen"))
    every_set = lax.all_gather(set_grads, "trade", axis=0, tiled=True)
    trade_grads = jnp.take(every_set, positions, axis=0)
    flow_grads = jnp.take_along_axis(trade_grads, coupon_dates, axis=1)
    return (credit_charge, flow_grads)


def solution(mesh):
    in_specs = (
        P("trade", None),
        P("trade", None),
        P("trade"),
        P(),
        P("trade"),
        P("trade"),
        P("trade"),
        P("date", None, ("groups", "scen")),
        P(None, "date"),
        P(),
        P(),
    )
    out_specs = (P("groups"), P(("groups", "trade"), None))
    return jax.shard_map(
        per_device, mesh=mesh, in_specs=in_specs, out_specs=out_specs, check_vma=False
    )
```

profile of v0, /device:TPU:0, one launch (start us, length us, event | category | flops | bytes accessed | tf_op | source)
XLA Modules:
  0.0 241.7 jit_solution(6793419968518047807)
XLA Ops:
  7.2 0.0 copy-start
  7.2 0.0 copy-start.6
  7.2 0.0 copy-start.10
  7.2 0.0 copy-start.9
  7.2 0.0 copy-start.5
  7.2 0.0 reduce-scatter.2.cloned.1.call-start
  7.3 1.1 copy.25
  8.4 0.0 copy-start.8
  8.4 0.9 copy.26
  9.2 5.7 %while.11 = (s32[]{:T(128)}, bf16[2,128,128]{2,1,0:T(8,128)(2,1)S(1)}, s32[2,128,64]{2,1,0:T(8,128)S(1)}, bf16[2,128,64]{2,1,0:T(8,128)(2,1)S(1)}, s32[]{:T(128)}) while((s32[]{:T(128)}, bf16[2,128,128]{2,1,0:T(8,128)(2,1)S(1)}, s32[2,128,64]{2,1,0:T(8,128)S(1)}, bf16[2,128,64]{2,1,0:T(8,128)(2,1)S(1)}, s32[]{:T(128)}) %tuple.46), condition=%wide.region_2.3_spmd.clone, body=%wide.region_0.0_spmd.clone.sunk | while | flops 3137538 | bytes 278609 | solution.py:38
  9.3 2.8 %select_reduce_fusion.2 = bf16[128,128]{1,0:T(8,128)(2,1)S(1)} fusion(f32[128,64]{1,0:T(8,128)S(1)} %bitcast_convert_fusion.2, s32[128,64]{1,0:T(8,128)S(1)} %dynamic-slice_bitcast_fusion.2), kind=kLoop, calls=%fused_computation.5.clone.1 | loop fusion | flops 3129344 | bytes 98304 | tf_op jit(solution)/shard_map/while/body/eval_jaxpr/reduce_sum | solution.py:30
  12.2 2.8 %select_reduce_fusion.2 = bf16[128,128]{1,0:T(8,128)(2,1)S(1)} fusion(f32[128,64]{1,0:T(8,128)S(1)} %bitcast_convert_fusion.2, s32[128,64]{1,0:T(8,128)S(1)} %dynamic-slice_bitcast_fusion.2), kind=kLoop, calls=%fused_computation.5.clone.1 | loop fusion | flops 3129344 | bytes 98304 | tf_op jit(solution)/shard_map/while/body/eval_jaxpr/reduce_sum | solution.py:30
  15.0 0.7 compare_select_fusion.4
  15.7 2.0 gather_fusion
  17.7 0.7 compare_and_fusion
  18.4 0.9 fusion.25
  19.3 0.0 reduce-scatter.2.cloned.1.call-update
  19.3 0.0 all-reduce.8.cloned.1.call-start
  19.4 0.0 copy-done.6
  19.4 0.1 iota_compare_fusion.7
  19.5 0.1 broadcast_compare_fusion
  19.6 0.0 copy-done.10
  19.6 0.0 copy-done.9
  19.6 0.0 copy-done.5
  19.6 2.7 %broadcast_select_fusion.5 = bf16[64,128,128]{2,1,0:T(8,128)(2,1)} fusion(bf16[64,128,128]{2,1,0:T(8,128)(2,1)S(1)} %copy-done.5, pred[64,128]{1,0:T(8,128)(4,1)S(1)} %iota_compare_fusion.7), kind=kLoop, calls=%fused_computation.44 | loop fusion | flops 1048576 | bytes 4202496 | tf_op jit(solution)/shard_map/jit(_where)/select_n | solution.py:91
  22.3 0.0 copy-done.8
  22.3 0.2 fusion.27
  22.5 3.3 %copy.27 = bf16[64,128,128]{1,2,0:T(8,128)(2,1)S(1)} copy(bf16[64,128,128]{2,1,0:T(8,128)(2,1)} %broadcast_select_fusion.5) | data formatting | bytes 4194304 | tf_op jit(solution)/shard_map/jit(_where)/select_n | solution.py:91
  25.8 0.0 copy-done
  25.8 0.3 broadcast_multiply_fusion
  26.1 15.6 %reduce-scatter.2.cloned.1.call-done = f32[128,128]{1,0:T(8,128)} async-done(((f32[512,128]{1,0:T(8,128)}), f32[128,128]{1,0:T(8,128)}) %reduce-scatter.2.cloned.1.call-update) | async-done | bytes 65552 | tf_op jit(solution)/shard_map/reduce_scatter | solution.py:81
  41.8 0.0 copy-start.7
  41.8 1.6 fusion.29
  43.3 0.0 copy-start.1
  43.4 3.5 %collective-permute-start = (bf16[128,4,128]{0,2,1:T(8,128)(2,1)S(1)}, bf16[128,4,128]{0,2,1:T(8,128)(2,1)S(1)}, u32[]{:S(2)}, u32[]{:S(2)}) collective-permute-start(bf16[128,4,128]{0,2,1:T(8,128)(2,1)S(1)} %slice.97), channel_id=1, source_target_pairs={{0,2},{1,3},{4,6},{5,7},{8,10},{9,11},{12,14},{13,15},{16,18},{17,... | collective-permute-start | bytes 393224 | tf_op jit(solution)/shard_map/ppermute | solution.py:15
  46.9 0.0 copy-done.1
  46.9 0.1 reshape.143
  47.0 2.4 collective-permute-done
  49.4 0.0 copy-done.7
  49.4 12.9 %broadcast_select_fusion.3 = (f32[128,64,128]{0,2,1:T(8,128)S(1)}, f32[128,64,128]{0,2,1:T(8,128)}, f32[128,64,128]{0,2,1:T(8,128)}) fusion(pred[128]{0:T(512)(128)(4,1)S(1)} %get-tuple-element.64, f32[128,64,128]{0,2,1:T(8,128)} %bitcast.49, f32[128,64]{0,1:T(8,128)S(1)} %get-tuple-element.66, pred[128,64]{0,1:T(8,128)(4,1)S(1)} %broadcast_compare_fusion, ...), kind=kLoop, calls=%fused_computation.42 | loop fusion | flops 33554432 | bytes 17081472 | tf_op jit(solution)/shard_map/jit(_where)/select_n | solution.py:134
  62.3 7.7 %broadcast_select_fusion.2 = (f32[128,64,128]{0,2,1:T(8,128)S(1)}, f32[128,64,128]{0,2,1:T(8,128)}, f32[128,64,128]{0,2,1:T(8,128)}, f32[128,64,128]{0,2,1:T(8,128)}) fusion(f32[128,64,128]{0,2,1:T(8,128)} %get-tuple-element.55, pred[128]{0:T(512)(128)(4,1)S(1)} %get-tuple-element.65, pred[128]{0:T(512)(128)(4,1)S(1)} %get-tuple-element.63, ...), kind=kLoop, calls=%fused_computation.41 | loop fusion | flops 4194304 | bytes 20972032 | tf_op jit(solution)/shard_map/jit(_where)/select_n | solution.py:134
  70.0 0.0 copy-start.2
  70.0 0.0 copy-start.3
  70.0 6.1 %pad_add_fusion = f32[128,68,128]{0,2,1:T(8,128)S(1)} fusion(f32[128,64,128]{0,2,1:T(8,128)} %get-tuple-element.60, f32[128,64,128]{0,2,1:T(8,128)} %get-tuple-element.58, f32[128,64,128]{0,2,1:T(8,128)} %get-tuple-element.59, f32[128,64,128]{0,2,1:T(8,128)S(1)} %get-tuple-element.57, f32[128,64,128]{0,2,1:T(8,128)S(1)} %get-tuple-element.54), kind=kLoop, calls=%fused_computation.14 | loop fusion | flops 4456448 | bytes 25427968 | tf_op jit(solution)/shard_map/add | solution.py:135
  76.2 1.5 collective-permute-start.1
  77.7 0.0 copy-done.2
  77.7 0.0 copy-done.3
  77.7 0.0 copy-start.4
  77.7 5.4 %fusion.15 = f32[128,64]{0,1:T(8,128)S(1)} fusion(f32[128,64,128]{0,2,1:T(8,128)S(1)} %copy-done.3, pred[128,64]{0,1:T(8,128)(4,1)S(1)} %broadcast_compare_fusion, f32[128,8192]{0,1:S(1)} %copy-done.2), kind=kLoop, calls=%fused_computation.28 | loop fusion | flops 18866176 | bytes 8429568 | tf_op jit(solution)/shard_map/reduce_sum | solution.py:110
  83.1 0.0 collective-permute-done.1
  83.1 0.0 copy-done.4
  83.1 4.5 %fusion.22 = f32[128,128]{1,0:T(8,128)} fusion(bf16[64,128,128]{2,1,0:T(8,128)(2,1)S(1)} %copy-done.4, f32[128,68,128]{0,2,1:T(8,128)S(1)} %pad_add_fusion, bf16[128,4,128]{0,2,1:T(8,128)(2,1)S(1)} %collective-permute-done.1, f32[128,64]{0,1:T(8,128)S(1)} %get-tuple-element.66, f32[128,64,128]{0,2,1:T(8,128)S(1)} %bitcast.50, ...), kind=kOutput, calls=%fused_computation.45 | convolution fusion | flops 287309824 | bytes 14917632 | tf_op jit(solution)/shard_map/pts,tus->pu/dot_general | solution.py:141
  87.6 0.0 all-reduce.8.cloned.1.call-update
  87.6 0.2 convolution_bitcast_fusion
  87.8 30.0 %psum.14 = f32[128]{0:T(128)} all-reduce(f32[128]{0:T(128)S(1)} %convolution_bitcast_fusion), channel_id=1, replica_groups=mesh['groups'=2,'trade'=4,'date'=2,'scen'=2] {'trade','date','scen'}, use_global_device_ids=true, to_apply=%region_6.7 | all-reduce | flops 128 | bytes 1024 | tf_op jit(solution)/shard_map/psum | solution.py:128
  117.8 0.4 all-reduce.8.cloned.1.call-done
  118.3 14.0 %all_gather.3 = f32[512,128]{1,0:T(8,128)S(1)} all-gather(f32[128,128]{1,0:T(8,128)} %all-reduce.8.cloned.1.call-done), channel_id=1, replica_groups=mesh['groups'=2,'trade'=4,'date'=2,'scen'=2] {'trade'}, dimensions={0}, use_global_device_ids=true | all-gather | bytes 327680 | tf_op jit(solution)/shard_map/all_gather | solution.py:145
  132.3 0.7 gather_fusion.1
  133.0 0.1 broadcast_select_fusion.6
  133.2 100.8 %gather_fusion.2 = f32[16384]{0:T(1024)S(1)} fusion(f32[256,128]{1,0:T(8,128)S(1)} %broadcast_select_fusion.6, s32[16384]{0:T(1024)S(1)} %reshape.143), kind=kCustom, calls=%fused_computation.2 | custom fusion | bytes 262144 | tf_op jit(solution)/shard_map/jit(take_along_axis)/gather | solution.py:147
  234.0 0.1 reshape.146
  234.1 0.7 copy.32
  (20 shorter events, 0.3 us)
Async XLA Ops:
  7.2 18.6 %copy-start = (f32[128,64]{0,1:T(8,128)S(1)}, f32[128,64]{0,1:T(8,128)}, u32[]{:S(2)}) copy-start(f32[128,64]{0,1:T(8,128)} %param.21) | copy-start | bytes 98308
  7.2 12.2 %copy-start.6 = (s32[128]{0:T(128)S(1)}, s32[128]{0:T(128)}, u32[]{:S(2)}) copy-start(s32[128]{0:T(128)} %param.17) | copy-start | bytes 1540
  7.2 12.4 %copy-start.10 = (f32[128]{0:T(128)S(1)}, f32[128]{0:T(128)}, u32[]{:S(2)}) copy-start(f32[128]{0:T(128)} %param.22) | copy-start | bytes 1540
  7.2 12.4 %copy-start.9 = (f32[128]{0:T(128)S(1)}, f32[128]{0:T(128)}, u32[]{:S(2)}) copy-start(f32[128]{0:T(128)} %param.23) | copy-start | bytes 1540
  7.2 12.4 %copy-start.5 = (bf16[64,128,128]{2,1,0:T(8,128)(2,1)S(1)}, bf16[64,128,128]{2,1,0:T(8,128)(2,1)}, u32[]{:S(2)}) copy-start(bf16[64,128,128]{2,1,0:T(8,128)(2,1)} %param.20) | copy-start | bytes 6291460
  7.2 34.6 %reduce-scatter.2.cloned.1.call-start = ((), (), s32[]{:S(2)}) async-start(), calls=%async_computation.1 | async-start | bytes 327680 | tf_op jit(solution)/shard_map/reduce_scatter | solution.py:81
  8.4 13.9 %copy-start.8 = (s32[128]{0:T(128)S(1)}, s32[128]{0:T(128)}, u32[]{:S(2)}) copy-start(s32[128]{0:T(128)} %param.19) | copy-start | bytes 1540
  19.3 98.9 %all-reduce.8.cloned.1.call-start = ((), (), s32[]{:S(2)}) async-start(), calls=%async_computation.2 | async-start | bytes 131072 | tf_op jit(solution)/shard_map/psum | solution.py:144
  41.8 7.6 %copy-start.7 = (f32[128]{0:T(128)S(1)}, f32[128]{0:T(128)}, u32[]{:S(2)}) copy-start(f32[128]{0:T(128)} %param.18) | copy-start | bytes 1540
  43.3 3.5 %copy-start.1 = (f32[128,8192]{0,1}, f32[128,8192]{0,1:S(1)}, u32[]{:S(2)}) copy-start(f32[128,8192]{0,1:S(1)} %fusion.29) | copy-start | bytes 12582916
  43.4 6.0 %collective-permute-start = (bf16[128,4,128]{0,2,1:T(8,128)(2,1)S(1)}, bf16[128,4,128]{0,2,1:T(8,128)(2,1)S(1)}, u32[]{:S(2)}, u32[]{:S(2)}) collective-permute-start(bf16[128,4,128]{0,2,1:T(8,128)(2,1)S(1)} %slice.97), channel_id=1, source_target_pairs={{0,2},{1,3},{4,6},{5,7},{8,10},{9,11},{12,14},{13,15},{16,18},{17,... | collective-permute-start | bytes 393224 | tf_op jit(solution)/shard_map/ppermute | solution.py:15
  70.0 7.7 %copy-start.2 = (f32[128,8192]{0,1:S(1)}, f32[128,8192]{0,1}, u32[]{:S(2)}) copy-start(f32[128,8192]{0,1} %copy-done.1) | copy-start | bytes 12582916
  70.0 7.7 %copy-start.3 = (f32[128,64,128]{0,2,1:T(8,128)S(1)}, f32[128,64,128]{0,2,1:T(8,128)}, u32[]{:S(2)}) copy-start(f32[128,64,128]{0,2,1:T(8,128)} %get-tuple-element.56) | copy-start | bytes 12582916
  76.2 6.9 %collective-permute-start.1 = (bf16[128,4,128]{0,2,1:T(8,128)(2,1)S(1)}, bf16[128,4,128]{0,2,1:T(8,128)(2,1)S(1)}, u32[]{:S(2)}, u32[]{:S(2)}) collective-permute-start(bf16[128,4,128]{0,2,1:T(8,128)(2,1)S(1)} %slice.96), channel_id=1, source_target_pairs={{2,0},{3,1},{6,4},{7,5},{10,8},{11,9},{14,12},{15,13},{18,16},{19,... | collective-permute-start | bytes 393224 | tf_op jit(solution)/shard_map/ppermute | solution.py:15
  77.7 5.4 %copy-start.4 = (bf16[64,128,128]{2,1,0:T(8,128)(2,1)S(1)}, bf16[64,128,128]{2,1,0:T(8,128)(2,1)}, u32[]{:S(2)}) copy-start(bf16[64,128,128]{2,1,0:T(8,128)(2,1)} %broadcast_select_fusion.5) | copy-start | bytes 6291460
Sparse Core Ops, SparseCore 0:
  19.5 22.2 reduce-scatter.1
  87.8 30.4 all-reduce.7
where the time goes:
time: 242 us
  local copies, waits for them, and re-layouts  110 us (45%)
  blocking collectives  44 us (18%)
  other arithmetic  42.2 us (17%)
  waiting for transfers between devices  18.5 us (8%)
  between operations  14.4 us (6%)
  matrix products  7.66 us (3%)
  starting transfers between devices  5.02 us (2%)
    gather x3, local copies, waits for them, and re-layouts, per_device(): flow_grads = jnp.take_along_axis(trade_grads, coupon_dates, axis=1)  101 us
    psum x1, blocking collectives, per_device(): credit_charge = lax.psum(partial_charge, ('trade', 'date', 'scen'))  30 us
    select_n x2, other arithmetic, per_device(): picked = jnp.where(lag_rows == offset, backward, jnp.float32(0.0))  20.6 us
    reduce_scatter x1, waiting for transfers between devices, per_device(): lax.psum_scatter(jnp.dot(member, trade_flows, preferred_element_type=jnp....  15.6 us
    all_gather x1, blocking collectives, per_device(): every_set = lax.all_gather(set_grads, 'trade', axis=0, tiled=True)  14 us
    add x1, other arithmetic, per_device(): carried + jnp.pad(picked, ((0, 0), (LAGMAX - offset, offset), (0, 0)))  6.13 us
    reduce_sum x2, other arithmetic, per_block(): jnp.sum(jnp.where(matched, amounts.astype(jnp.float32)[:, :, None], jnp.f...  5.58 us
    reduce_sum x1, other arithmetic, per_device(): exposure_curve = jnp.sum(exposure, axis=2)  5.36 us
  transfers between devices with their start and end apart: 4, of which 3 were waited for; matrix products, arithmetic and copies ran while one was open for 5% of the time, Pallas kernels for 0%

commit v1 on v0

v1 whole, which is shorter than its diff:
```python
import functools

import jax
import jax.numpy as jnp
from jax import lax
from jax.experimental import pallas as pl
from jax.experimental.pallas import tpu as pltpu
from jax.sharding import PartitionSpec as P

LAGMAX = 4
RATE = 10.0
STEP = 4
MESH = pl.DeviceIdType.MESH
NT = (((1,), (1,)), ((), ()))
F32 = jnp.float32
BF16 = jnp.bfloat16


def smooth(a):
    s = 0.5 + 0.5 * jnp.tanh(0.5 * jnp.abs(a))
    return jnp.maximum(a, 0.0) - jnp.log(s), jnp.where(a >= 0.0, s, 1.0 - s)


def exact_dot(a, b, dims=(((1,), (0,)), ((), ()))):
    return lax.dot_general(a, b, dims, precision=lax.Precision.HIGHEST, preferred_element_type=F32)


def kernel(
    n_trade,
    n_date,
    n_scen,
    cash_ref,
    dates_ref,
    sets_ref,
    slots_ref,
    lags_ref,
    limits_ref,
    cpty_ref,
    probs_ref,
    loss_ref,
    cot_ref,
    market_ref,
    charge_ref,
    flows_ref,
    fwd,
    fwd_t,
    vals,
    coll,
    gate,
    direct,
    hazard,
    weight,
    member,
    parts_out,
    parts_in,
    set_flows,
    total,
    total_in,
    every,
    trade_rows,
    charge_out,
    charge_in,
    charge_sum,
    charge_far,
    load_sem,
    halo_sem,
    parts_sem,
    flow_sem,
    total_sem,
    charge_sem,
    far_sem,
    every_z_sem,
    every_g_sem,
):
    z = lax.axis_index("trade")
    d = lax.axis_index("date")
    c = lax.axis_index("scen")
    n_group = n_date * n_scen
    g = d * n_scen + c
    span, n_u, n_s = market_ref.shape
    n_p = lags_ref.shape[1]
    n_sets = slots_ref.shape[1]
    n_c = probs_ref.shape[1]
    n_n = sets_ref.shape[1]
    n_k = dates_ref.shape[0]
    uq = n_u // n_group
    steps = span + LAGMAX
    first = d * span

    def trade_peer(k):
        return {"trade": lax.rem(z + k, n_trade)}

    def group_peer(k):
        peer = lax.rem(g + k, n_group)
        return {"date": peer // n_scen, "scen": lax.rem(peer, n_scen)}

    def send(src, dst, sems, index, device):
        copy = pltpu.make_async_remote_copy(
            src_ref=src,
            dst_ref=dst,
            send_sem=sems.at[(0,) + index],
            recv_sem=sems.at[(1,) + index],
            device_id=device,
            device_id_type=MESH,
        )
        copy.start()
        return copy

    barrier = pltpu.get_barrier_semaphore()
    for k in range(1, n_trade):
        pl.semaphore_signal(barrier, inc=1, device_id=trade_peer(k), device_id_type=MESH)
    for k in range(1, n_group):
        pl.semaphore_signal(barrier, inc=1, device_id=group_peer(k), device_id_type=MESH)

    load = pltpu.make_async_copy(market_ref, fwd.at[pl.ds(LAGMAX, span)], load_sem)
    load.start()

    mine = pl.multiple_of(g * uq, uq)
    u_rows = lax.broadcasted_iota(jnp.int32, (uq, n_n), 0) + g * uq
    grid = jnp.zeros((uq, n_n), F32)
    cash = cash_ref[...].astype(F32)
    moments = dates_ref[...]
    for k in range(n_k):
        grid = jnp.where(u_rows == moments[k : k + 1, :], cash[k : k + 1, :], grid)

    wanted = lax.broadcasted_iota(jnp.int32, (n_sets, n_n), 0) == sets_ref[...]
    slots = slots_ref[...]
    digit = lax.broadcasted_iota(jnp.int32, (8, n_sets), 0)
    digits = jnp.where(digit == 0, slots >> 6, jnp.where(digit == 1, slots & 63, 0))
    found = jnp.dot(digits.astype(F32).astype(BF16), wanted.astype(F32).astype(BF16), preferred_element_type=F32)
    positions = (found[0:1, :] * 64.0 + found[1:2, :]).astype(jnp.int32)
    p_rows = lax.broadcasted_iota(jnp.int32, (n_sets, n_n), 0)
    member[...] = (p_rows == positions).astype(F32).astype(BF16)
    partial = lax.dot_general(grid.astype(BF16), member[...], NT, preferred_element_type=F32)
    for o in range(n_trade):
        parts_out[o] = partial[:, o * n_p : (o + 1) * n_p]

    pl.semaphore_wait(barrier, n_trade - 1 + n_group - 1)
    pending = []
    arrivals = []
    for k in range(1, n_trade):
        to = lax.rem(z + k, n_trade)
        arrivals.append(send(parts_out.at[to], parts_in.at[k], parts_sem, (k,), trade_peer(k)))
    next_date = {"date": lax.rem(d + 1, n_date)}
    halo = send(
        market_ref.at[pl.ds(span - LAGMAX, LAGMAX)], fwd.at[pl.ds(0, LAGMAX)], halo_sem, (), next_date
    )

    named = lax.broadcasted_iota(jnp.int32, (n_c, n_p), 0) == cpty_ref[...]
    named = named.astype(F32)
    loss = loss_ref[...]
    scale_row = lax.broadcasted_iota(jnp.int32, (8, n_c), 0)
    scales = jnp.where(scale_row == 0, loss, jnp.where(scale_row == 1, loss * cot_ref[...], 0.0))
    scales = exact_dot(scales, named)
    paths = float(n_s * n_scen)
    hazard[...] = exact_dot(probs_ref[...], named)
    weight[...] = hazard[...] * (scales[1:2, :] / paths)

    u_col = lax.broadcasted_iota(jnp.int32, (n_u, n_s), 0)

    def mask_dates(t, shown):
        later = (u_col > first + (t - LAGMAX)).astype(F32) * shown
        block = fwd[t] * later.astype(BF16)
        fwd[t] = block
        fwd_t[t] = block.T

    load.wait()

    def mask_step(i, carry):
        for b in range(STEP):
            mask_dates(LAGMAX + i * STEP + b, 1.0)
        return carry

    lax.fori_loop(0, span // STEP, mask_step, 0)

    for copy in arrivals:
        copy.wait_recv()
    pending += arrivals
    mine_sum = parts_out[z]
    for k in range(1, n_trade):
        mine_sum = mine_sum + parts_in[k]
    set_flows[pl.ds(mine, uq), :] = mine_sum.astype(BF16)
    arrivals = []
    for k in range(1, n_group):
        block = set_flows.at[pl.ds(mine, uq)]
        arrivals.append(send(block, block, flow_sem, (k,), group_peer(k)))

    halo.wait()
    after_first = jnp.where(d > 0, 1.0, 0.0).astype(F32)
    for b in range(LAGMAX):
        mask_dates(b, after_first)
    for copy in arrivals:
        copy.wait_recv()
    pending += arrivals

    flows = set_flows[...]
    limits = limits_ref[...] * RATE

    def value_date(t, shown):
        v = jnp.dot(fwd_t[t], flows, preferred_element_type=F32) * RATE
        amount, slope = smooth(v - limits)
        if shown is not None:
            amount, slope = amount * shown, slope * shown
        vals[t] = v
        coll[t] = amount
        gate[t] = slope

    for b in range(LAGMAX):
        value_date(b, after_first)

    def value_step(i, carry):
        for b in range(STEP):
            value_date(LAGMAX + i * STEP + b, None)
        return carry

    lax.fori_loop(0, span // STEP, value_step, 0)

    lags = lags_ref[...]

    def by_lag(rows):
        out = rows[0]
        for lag in range(1, LAGMAX + 1):
            out = jnp.where(lags == lag, rows[lag], out)
        return out

    for b in range(LAGMAX):
        direct[b] = jnp.zeros((n_s, n_p), F32)
        direct[steps + b] = jnp.zeros((n_s, n_p), F32)

    def exposure_step(i, acc):
        for b in range(STEP):
            own = i * STEP + b
            t = LAGMAX + own
            margin = vals[t] - by_lag([coll[t - lag] for lag in range(LAGMAX + 1)])
            amount, slope = smooth(margin)
            acc = acc + amount * hazard[pl.ds(own, 1), :]
            direct[t] = slope * weight[pl.ds(own, 1), :]
        return acc

    acc = lax.fori_loop(0, span // STEP, exposure_step, jnp.zeros((n_s, n_p), F32))
    terms = jnp.sum(acc, axis=0, keepdims=True) * (scales[0:1, :] * (1.0 / (RATE * paths)))
    charge_out[...] = exact_dot(jnp.broadcast_to(terms, (8, n_p)), named, NT)
    charges = []
    for k in range(1, n_group):
        charges.append(send(charge_out, charge_in.at[k], charge_sem, (k,), group_peer(k)))

    def grad_step(i, acc):
        for b in range(STEP):
            t = i * STEP + b
            later = by_lag([direct[t + lag] for lag in range(LAGMAX + 1)])
            block = (direct[t] - later * gate[t]).astype(BF16)
            acc = acc + jnp.dot(fwd[t], block, preferred_element_type=F32)
        return acc

    total[...] = lax.fori_loop(0, steps // STEP, grad_step, jnp.zeros((n_u, n_p), F32))

    arrivals = []
    for k in range(1, n_group):
        theirs = pl.multiple_of(lax.rem(g + k, n_group) * uq, uq)
        arrivals.append(
            send(total.at[pl.ds(theirs, uq)], total_in.at[k], total_sem, (k,), group_peer(k))
        )

    for copy in charges:
        copy.wait_recv()
    pending += charges
    group_charge = charge_out[...]
    for k in range(1, n_group):
        group_charge = group_charge + charge_in[k]
    charge_sum[...] = group_charge
    charges = []
    for k in range(1, n_trade):
        charges.append(send(charge_sum, charge_far.at[k], far_sem, (k,), trade_peer(k)))

    for copy in arrivals:
        copy.wait_recv()
    pending += arrivals
    mine_sum = total[pl.ds(mine, uq), :]
    for k in range(1, n_group):
        mine_sum = mine_sum + total_in[k]
    every[z, pl.ds(mine, uq), :] = mine_sum.astype(BF16)

    across = []
    block = every.at[z, pl.ds(mine, uq)]
    for k in range(1, n_trade):
        across.append(send(block, block, every_z_sem, (k,), trade_peer(k)))
    within = []
    for k in range(1, n_group):
        within.append(send(block, block, every_g_sem, (0, k), group_peer(k)))
    for j in range(1, n_trade):
        across[j - 1].wait_recv()
        block = every.at[lax.rem(z + n_trade - j, n_trade), pl.ds(mine, uq)]
        for k in range(1, n_group):
            within.append(send(block, block, every_g_sem, (j, k), group_peer(k)))
    pending += across

    for copy in charges:
        copy.wait_recv()
    pending += charges
    group_charge = charge_sum[...]
    for k in range(1, n_trade):
        group_charge = group_charge + charge_far[k]
    charge_ref[...] = group_charge[0:1, :]

    for copy in within:
        copy.wait_recv()
    pending += within
    rows = jnp.zeros((n_u, n_n), F32)
    for o in range(n_trade):
        rows = rows + jnp.dot(every[o], member[o * n_p : (o + 1) * n_p, :], preferred_element_type=F32)
    trade_rows[...] = rows

    def pick_step(i, out):
        base = pl.multiple_of(i * 8, 8)
        rows = trade_rows[pl.ds(base, 8), :]
        for b in range(8):
            out = jnp.where(moments == base + b, rows[b : b + 1, :], out)
        return out

    flows_ref[...] = lax.fori_loop(0, n_u // 8, pick_step, jnp.zeros((n_k, n_n), F32))
    for copy in pending:
        copy.wait_send()


def per_device(
    cash_flows,
    coupon_dates,
    trade_sets,
    set_slots,
    set_lags,
    thresholds,
    set_cpty,
    discounts,
    default_probs,
    loss_given,
    cva_cotangent,
):
    n_trade, n_date, n_scen = (lax.axis_size(a) for a in ("trade", "date", "scen"))
    n_group = n_date * n_scen
    n_n, n_k = cash_flows.shape
    span, n_u, n_s = discounts.shape
    n_p = set_lags.shape[0]
    n_sets = set_slots.shape[0]
    n_c = loss_given.shape[0]
    uq = n_u // n_group
    steps = span + LAGMAX
    vmem = pl.BlockSpec(memory_space=pltpu.VMEM)
    dma = pltpu.SemaphoreType.DMA
    charge, flow_grads = pl.pallas_call(
        functools.partial(kernel, n_trade, n_date, n_scen),
        out_shape=(
            jax.ShapeDtypeStruct((1, n_c), F32),
            jax.ShapeDtypeStruct((n_k, n_n), F32),
        ),
        in_specs=[vmem] * 10 + [pl.BlockSpec(memory_space=pl.ANY)],
        out_specs=(vmem, vmem),
        scratch_shapes=[
            pltpu.VMEM((steps, n_u, n_s), BF16),
            pltpu.VMEM((steps, n_s, n_u), BF16),
            pltpu.VMEM((steps, n_s, n_p), F32),
            pltpu.VMEM((steps, n_s, n_p), F32),
            pltpu.VMEM((steps, n_s, n_p), F32),
            pltpu.VMEM((steps + LAGMAX, n_s, n_p), F32),
            pltpu.VMEM((span, n_p), F32),
            pltpu.VMEM((span, n_p), F32),
            pltpu.VMEM((n_sets, n_n), BF16),
            pltpu.VMEM((n_trade, uq, n_p), F32),
            pltpu.VMEM((n_trade, uq, n_p), F32),
            pltpu.VMEM((n_u, n_p), BF16),
            pltpu.VMEM((n_u, n_p), F32),
            pltpu.VMEM((n_group, uq, n_p), F32),
            pltpu.VMEM((n_trade, n_u, n_p), BF16),
            pltpu.VMEM((n_u, n_n), F32),
            pltpu.VMEM((8, n_c), F32),
            pltpu.VMEM((n_group, 8, n_c), F32),
            pltpu.VMEM((8, n_c), F32),
            pltpu.VMEM((n_trade, 8, n_c), F32),
            dma,
            dma((2,)),
            dma((2, n_trade)),
            dma((2, n_group)),
            dma((2, n_group)),
            dma((2, n_group)),
            dma((2, n_trade)),
            dma((2, n_trade)),
            dma((2, n_trade, n_group)),
        ],
        compiler_params=pltpu.CompilerParams(
            collective_id=0, has_side_effects=True, vmem_limit_bytes=48 * 1024 * 1024
        ),
    )(
        cash_flows.T,
        coupon_dates.T,
        trade_sets.reshape(1, -1),
        set_slots.reshape(1, -1),
        set_lags.reshape(1, -1),
        thresholds.reshape(1, -1),
        set_cpty.reshape(1, -1),
        default_probs.T,
        loss_given.reshape(1, -1),
        cva_cotangent.reshape(1, -1),
        discounts,
    )
    return charge.reshape(-1), flow_grads.T


def solution(mesh):
    in_specs = (
        P("trade", None),
        P("trade", None),
        P("trade"),
        P(),
        P("trade"),
        P("trade"),
        P("trade"),
        P("date", None, ("groups", "scen")),
        P(None, "date"),
        P(),
        P(),
    )
    out_specs = (P("groups"), P(("groups", "trade"), None))
    return jax.shard_map(
        per_device, mesh=mesh, in_specs=in_specs, out_specs=out_specs, check_vma=False
    )
```

time: 242 us -> 45.3 us (0.19)
  local copies, waits for them, and re-layouts: 110 us -> 9.71 us
  blocking collectives: 44 us -> 0 us
  other arithmetic: 42.2 us -> 0 us
  Pallas kernels: 0 us -> 34.5 us
  waiting for transfers between devices: 18.5 us -> 0 us
  between operations: 14.4 us -> 0.66 us
  matrix products: 7.66 us -> 0 us
  starting transfers between devices: 5.02 us -> 0 us
    gather x5 -> x0, local copies, waits for them, and re-layouts: 104 us -> none  [the longest x3 101 us: per_device(): flow_grads = jnp.take_along_axis(trade_grads, coupon_dates, axis=1)]
    pallas_call x0 -> x1, Pallas kernels: none -> 34.5 us  [per_device(): pl.pallas_call(functools.partial(kernel, n_trade, n_date, n_scen), out_sh...]
    psum x1 -> x0, blocking collectives: 30 us -> none  [per_device(): credit_charge = lax.psum(partial_charge, ('trade', 'date', 'scen'))]
    select_n x7 -> x0, other arithmetic: 24.1 us -> none  [the longest x2 20.6 us: per_device(): picked = jnp.where(lag_rows == offset, backward, jnp.float32(0.0))]
    reduce_scatter x1 -> x0, waiting for transfers between devices: 15.6 us -> none  [per_device(): lax.psum_scatter(jnp.dot(member, trade_flows, preferred_element_type=jnp....]
    all_gather x1 -> x0, blocking collectives: 14 us -> none  [per_device(): every_set = lax.all_gather(set_grads, 'trade', axis=0, tiled=True)]
    reduce_sum x4 -> x0, other arithmetic: 11 us -> none  [the longest x2 5.58 us: per_block(): jnp.sum(jnp.where(matched, amounts.astype(jnp.float32)[:, :, None], jnp.f...]
    unnamed x25 -> x24, local copies, waits for them, and re-layouts: 2.72 us -> 9.71 us
  transfers between devices with their start and end apart: 4 -> 0, of which waited for: 3 -> 0; matrix products, arithmetic and copies ran while one was open for 5% -> 0% of each run, Pallas kernels for 0% -> 0%
where the time goes in v1:
time: 45.3 us; the launch traced here: 44.9 us
  Pallas kernels  34.5 us (76%)
  local copies, waits for them, and re-layouts  9.71 us (21%)
  between operations  0.66 us (1%)
    pallas_call x1, Pallas kernels, per_device(): pl.pallas_call(functools.partial(kernel, n_trade, n_date, n_scen), out_sh...  34.5 us
    unnamed x24, local copies, waits for them, and re-layouts  9.71 us

profile of v1, /device:TPU:0, one launch (start us, length us, event | category | flops | bytes accessed | tf_op | source)
XLA Modules:
  0.0 44.9 jit_solution(7580706826929243576)
XLA Ops:
  0.6 0.0 copy-start
  0.6 1.6 %copy-done = bf16[64,128,128]{2,1,0:T(8,128)(2,1)S(1)} copy-done((bf16[64,128,128]{2,1,0:T(8,128)(2,1)S(1)}, bf16[64,128,128]{2,1,0:T(8,128)(2,1)}, u32[]{:S(2)}) %copy-start) | copy-done | bytes 2097176
  2.2 0.0 copy-start.1
  2.2 0.8 %copy-done.1 = s32[256,64]{0,1:T(8,128)S(1)} copy-done((s32[256,64]{0,1:T(8,128)S(1)}, s32[256,64]{0,1:T(8,128)}, u32[]{:S(2)}) %copy-start.1) | copy-done | bytes 65560
  3.1 0.0 copy-start.2
  3.1 0.8 %copy-done.2 = bf16[256,64]{0,1:T(8,128)(2,1)S(1)} copy-done((bf16[256,64]{0,1:T(8,128)(2,1)S(1)}, bf16[256,64]{0,1:T(8,128)(2,1)}, u32[]{:S(2)}) %copy-start.2) | copy-done | bytes 32792
  3.8 0.0 copy-start.3
  3.8 0.8 %copy-done.3 = f32[128,64]{0,1:T(8,128)S(1)} copy-done((f32[128,64]{0,1:T(8,128)S(1)}, f32[128,64]{0,1:T(8,128)}, u32[]{:S(2)}) %copy-start.3) | copy-done | bytes 32792
  4.6 0.0 copy-start.4
  4.6 0.7 %copy-done.4 = s32[512]{0:T(512)S(1)} copy-done((s32[512]{0:T(512)S(1)}, s32[512]{0:T(512)}, u32[]{:S(2)}) %copy-start.4) | copy-done | bytes 2072
  5.3 0.0 copy-start.5
  5.3 0.7 %copy-done.5 = s32[256]{0:T(256)S(1)} copy-done((s32[256]{0:T(256)S(1)}, s32[256]{0:T(256)}, u32[]{:S(2)}) %copy-start.5) | copy-done | bytes 1048
  5.9 0.0 copy-start.6
  5.9 0.7 %copy-done.6 = s32[128]{0:T(128)S(1)} copy-done((s32[128]{0:T(128)S(1)}, s32[128]{0:T(128)}, u32[]{:S(2)}) %copy-start.6) | copy-done | bytes 536
  6.6 0.0 copy-start.7
  6.6 0.7 %copy-done.7 = f32[128]{0:T(128)S(1)} copy-done((f32[128]{0:T(128)S(1)}, f32[128]{0:T(128)}, u32[]{:S(2)}) %copy-start.7) | copy-done | bytes 536
  7.3 0.0 copy-start.8
  7.3 0.7 %copy-done.8 = s32[128]{0:T(128)S(1)} copy-done((s32[128]{0:T(128)S(1)}, s32[128]{0:T(128)}, u32[]{:S(2)}) %copy-start.8) | copy-done | bytes 536
  7.9 0.0 copy-start.9
  7.9 0.7 %copy-done.9 = f32[128]{0:T(128)S(1)} copy-done((f32[128]{0:T(128)S(1)}, f32[128]{0:T(128)}, u32[]{:S(2)}) %copy-start.9) | copy-done | bytes 536
  8.6 0.0 copy-start.10
  8.6 0.7 %copy-done.10 = f32[128]{0:T(128)S(1)} copy-done((f32[128]{0:T(128)S(1)}, f32[128]{0:T(128)}, u32[]{:S(2)}) %copy-start.10) | copy-done | bytes 536
  9.2 34.5 %shard_map.122 = (f32[1,128]{1,0:T(1,128)S(1)}, f32[64,256]{1,0:T(8,128)S(1)}) custom-call(bf16[64,256]{1,0:T(8,128)(2,1)S(1)} %bitcast.14, s32[64,256]{1,0:T(8,128)S(1)} %bitcast.12, s32[1,256]{1,0:T(1,128)S(1)} %bitcast.17, s32[1,512]{1,0:T(1,128)S(1)} %bitcast.16, s32[1,128]{1,0:T(1,128)S(1)} %bitcast.18, f32[1,128]{1,0:T(1,128)S(1)} %bitcast.19, ...), custom_call_target="tpu_custom_call" | custom-call | tf_op jit(solution)/shard_map/pallas_call | solution.py:349
  43.7 0.5 %copy.15 = f32[128]{0:T(128)} copy(f32[128]{0:T(128)S(1)} %bitcast.23) | data formatting | bytes 1024
  44.2 0.6 %copy.16 = f32[256,64]{0,1:T(8,128)} copy(f32[256,64]{0,1:T(8,128)S(1)} %bitcast.13) | data formatting | bytes 131072
Async XLA Ops:
  0.6 1.6 %copy-start = (bf16[64,128,128]{2,1,0:T(8,128)(2,1)S(1)}, bf16[64,128,128]{2,1,0:T(8,128)(2,1)}, u32[]{:S(2)}) copy-start(bf16[64,128,128]{2,1,0:T(8,128)(2,1)} %market_ref.1) | copy-start | bytes 6291460
  2.2 0.8 %copy-start.1 = (s32[256,64]{0,1:T(8,128)S(1)}, s32[256,64]{0,1:T(8,128)}, u32[]{:S(2)}) copy-start(s32[256,64]{0,1:T(8,128)} %param.12) | copy-start | bytes 196612
  3.1 0.8 %copy-start.2 = (bf16[256,64]{0,1:T(8,128)(2,1)S(1)}, bf16[256,64]{0,1:T(8,128)(2,1)}, u32[]{:S(2)}) copy-start(bf16[256,64]{0,1:T(8,128)(2,1)} %param.11) | copy-start | bytes 98308
  3.8 0.8 %copy-start.3 = (f32[128,64]{0,1:T(8,128)S(1)}, f32[128,64]{0,1:T(8,128)}, u32[]{:S(2)}) copy-start(f32[128,64]{0,1:T(8,128)} %param.19) | copy-start | bytes 98308
  4.6 0.7 %copy-start.4 = (s32[512]{0:T(512)S(1)}, s32[512]{0:T(512)}, u32[]{:S(2)}) copy-start(s32[512]{0:T(512)} %param.14) | copy-start | bytes 6148
  5.3 0.7 %copy-start.5 = (s32[256]{0:T(256)S(1)}, s32[256]{0:T(256)}, u32[]{:S(2)}) copy-start(s32[256]{0:T(256)} %param.13) | copy-start | bytes 3076
  5.9 0.7 %copy-start.6 = (s32[128]{0:T(128)S(1)}, s32[128]{0:T(128)}, u32[]{:S(2)}) copy-start(s32[128]{0:T(128)} %param.15) | copy-start | bytes 1540
  6.6 0.7 %copy-start.7 = (f32[128]{0:T(128)S(1)}, f32[128]{0:T(128)}, u32[]{:S(2)}) copy-start(f32[128]{0:T(128)} %param.16) | copy-start | bytes 1540
  7.3 0.7 %copy-start.8 = (s32[128]{0:T(128)S(1)}, s32[128]{0:T(128)}, u32[]{:S(2)}) copy-start(s32[128]{0:T(128)} %param.17) | copy-start | bytes 1540
  7.9 0.7 %copy-start.9 = (f32[128]{0:T(128)S(1)}, f32[128]{0:T(128)}, u32[]{:S(2)}) copy-start(f32[128]{0:T(128)} %param.20) | copy-start | bytes 1540
  8.6 0.7 %copy-start.10 = (f32[128]{0:T(128)S(1)}, f32[128]{0:T(128)}, u32[]{:S(2)}) copy-start(f32[128]{0:T(128)} %param.21) | copy-start | bytes 1540

commit v2 on v1

--- a/solution.py
+++ b/solution.py
@@ -17,8 +17,8 @@
 
 
 def smooth(a):
-    s = 0.5 + 0.5 * jnp.tanh(0.5 * jnp.abs(a))
-    return jnp.maximum(a, 0.0) - jnp.log(s), jnp.where(a >= 0.0, s, 1.0 - s)
+    g = 0.5 + 0.5 * jnp.tanh(0.5 * a)
+    return jnp.maximum(a, 0.0) - jnp.log(jnp.maximum(g, 1.0 - g)), g
 
 
 def exact_dot(a, b, dims=(((1,), (0,)), ((), ()))):
@@ -29,6 +29,19 @@
     n_trade,
     n_date,
     n_scen,
+    cash_hbm,
+    dates_hbm,
+    sets_hbm,
+    slots_hbm,
+    lags_hbm,
+    limits_hbm,
+    cpty_hbm,
+    probs_hbm,
+    loss_hbm,
+    cot_hbm,
+    market_ref,
+    charge_ref,
+    flows_ref,
     cash_ref,
     dates_ref,
     sets_ref,
@@ -39,9 +52,6 @@
     probs_ref,
     loss_ref,
     cot_ref,
-    market_ref,
-    charge_ref,
-    flows_ref,
     fwd,
     fwd_t,
     vals,
@@ -63,14 +73,14 @@
     charge_sum,
     charge_far,
     load_sem,
+    small_sem,
     halo_sem,
     parts_sem,
     flow_sem,
     total_sem,
     charge_sem,
     far_sem,
-    every_z_sem,
-    every_g_sem,
+    every_sem,
 ):
     z = lax.axis_index("trade")
     d = lax.axis_index("date")
@@ -94,6 +104,11 @@
         peer = lax.rem(g + k, n_group)
         return {"date": peer // n_scen, "scen": lax.rem(peer, n_scen)}
 
+    others = [(j, k) for j in range(n_trade) for k in range(n_group) if j + k > 0]
+
+    def peer(j, k):
+        return {**trade_peer(j), **group_peer(k)}
+
     def send(src, dst, sems, index, device):
         copy = pltpu.make_async_remote_copy(
             src_ref=src,
@@ -107,13 +122,33 @@
         return copy
 
     barrier = pltpu.get_barrier_semaphore()
-    for k in range(1, n_trade):
-        pl.semaphore_signal(barrier, inc=1, device_id=trade_peer(k), device_id_type=MESH)
-    for k in range(1, n_group):
-        pl.semaphore_signal(barrier, inc=1, device_id=group_peer(k), device_id_type=MESH)
-
+    for j, k in others:
+        pl.semaphore_signal(barrier, inc=1, device_id=peer(j, k), device_id_type=MESH)
+
+    small = [
+        pltpu.make_async_copy(src, dst, small_sem.at[i])
+        for i, (src, dst) in enumerate(
+            (
+                (dates_hbm, dates_ref),
+                (cash_hbm, cash_ref),
+                (sets_hbm, sets_ref),
+                (slots_hbm, slots_ref),
+                (cpty_hbm, cpty_ref),
+                (loss_hbm, loss_ref),
+                (cot_hbm, cot_ref),
+                (probs_hbm, probs_ref),
+                (limits_hbm, limits_ref),
+                (lags_hbm, lags_ref),
+            )
+        )
+    ]
+    for copy in small:
+        copy.start()
     load = pltpu.make_async_copy(market_ref, fwd.at[pl.ds(LAGMAX, span)], load_sem)
     load.start()
+
+    for copy in small:
+        copy.wait()
 
     mine = pl.multiple_of(g * uq, uq)
     u_rows = lax.broadcasted_iota(jnp.int32, (uq, n_n), 0) + g * uq
@@ -135,7 +170,7 @@
     for o in range(n_trade):
         parts_out[o] = partial[:, o * n_p : (o + 1) * n_p]
 
-    pl.semaphore_wait(barrier, n_trade - 1 + n_group - 1)
+    pl.semaphore_wait(barrier, len(others))
     pending = []
     arrivals = []
     for k in range(1, n_trade):
@@ -196,63 +231,72 @@
     flows = set_flows[...]
     limits = limits_ref[...] * RATE
 
-    def value_date(t, shown):
-        v = jnp.dot(fwd_t[t], flows, preferred_element_type=F32) * RATE
-        amount, slope = smooth(v - limits)
-        if shown is not None:
-            amount, slope = amount * shown, slope * shown
-        vals[t] = v
-        coll[t] = amount
-        gate[t] = slope
-
-    for b in range(LAGMAX):
-        value_date(b, after_first)
-
-    def value_step(i, carry):
-        for b in range(STEP):
-            value_date(LAGMAX + i * STEP + b, None)
-        return carry
-
-    lax.fori_loop(0, span // STEP, value_step, 0)
-
     lags = lags_ref[...]
-
-    def by_lag(rows):
+    lags16 = lags.astype(F32).astype(BF16)
+
+    def by_lag(which, rows):
         out = rows[0]
         for lag in range(1, LAGMAX + 1):
-            out = jnp.where(lags == lag, rows[lag], out)
+            out = jnp.where(which == which.dtype.type(lag), rows[lag], out)
         return out
 
+    def value_block(i, shown=None):
+        for b in range(LAGMAX):
+            t = i * LAGMAX + b
+            v = jnp.dot(fwd_t[t], flows, preferred_element_type=F32) * RATE
+            amount, slope = smooth(v - limits)
+            if shown is not None:
+                amount, slope = amount * shown, slope * shown
+            vals[t] = v
+            coll[t] = amount
+            gate[t] = slope.astype(BF16)
+
+    def exposure_block(i, acc):
+        for b in range(LAGMAX):
+            t = i * LAGMAX + b
+            margin = vals[t] - by_lag(lags, [coll[t - lag] for lag in range(LAGMAX + 1)])
+            amount, slope = smooth(margin)
+            own = pl.ds(t - LAGMAX, 1)
+            acc = acc + jnp.sum(amount.reshape(-1, 8, n_p), axis=0) * hazard[own, :]
+            direct[t] = (slope * weight[own, :]).astype(BF16)
+        return acc
+
+    def grad_block(i):
+        out = None
+        for b in range(LAGMAX):
+            t = i * LAGMAX + b
+            later = by_lag(lags16, [direct[t + lag] for lag in range(LAGMAX + 1)])
+            block = direct[t] - later * gate[t]
+            term = jnp.dot(fwd[t], block, preferred_element_type=F32)
+            out = term if out is None else out + term
+        total[...] += out
+
     for b in range(LAGMAX):
-        direct[b] = jnp.zeros((n_s, n_p), F32)
-        direct[steps + b] = jnp.zeros((n_s, n_p), F32)
-
-    def exposure_step(i, acc):
-        for b in range(STEP):
-            own = i * STEP + b
-            t = LAGMAX + own
-            margin = vals[t] - by_lag([coll[t - lag] for lag in range(LAGMAX + 1)])
-            amount, slope = smooth(margin)
-            acc = acc + amount * hazard[pl.ds(own, 1), :]
-            direct[t] = slope * weight[pl.ds(own, 1), :]
+        direct[b] = jnp.zeros((n_s, n_p), BF16)
+        direct[steps + b] = jnp.zeros((n_s, n_p), BF16)
+    total[...] = jnp.zeros((n_u, n_p), F32)
+
+    last = steps // LAGMAX - 1
+    value_block(0, after_first)
+    value_block(1)
+    acc = exposure_block(1, jnp.zeros((8, n_p), F32))
+    value_block(2)
+
+    def block_step(i, acc):
+        grad_block(i - 3)
+        acc = exposure_block(i - 1, acc)
+        value_block(i)
         return acc
 
-    acc = lax.fori_loop(0, span // STEP, exposure_step, jnp.zeros((n_s, n_p), F32))
+    acc = lax.fori_loop(3, last + 1, block_step, acc)
+    acc = exposure_block(last, acc)
     terms = jnp.sum(acc, axis=0, keepdims=True) * (scales[0:1, :] * (1.0 / (RATE * paths)))
     charge_out[...] = exact_dot(jnp.broadcast_to(terms, (8, n_p)), named, NT)
     charges = []
     for k in range(1, n_group):
         charges.append(send(charge_out, charge_in.at[k], charge_sem, (k,), group_peer(k)))
-
-    def grad_step(i, acc):
-        for b in range(STEP):
-            t = i * STEP + b
-            later = by_lag([direct[t + lag] for lag in range(LAGMAX + 1)])
-            block = (direct[t] - later * gate[t]).astype(BF16)
-            acc = acc + jnp.dot(fwd[t], block, preferred_element_type=F32)
-        return acc
-
-    total[...] = lax.fori_loop(0, steps // STEP, grad_step, jnp.zeros((n_u, n_p), F32))
+    for i in range(last - 2, last + 1):
+        grad_block(i)
 
     arrivals = []
     for k in range(1, n_group):
@@ -280,20 +324,8 @@
         mine_sum = mine_sum + total_in[k]
     every[z, pl.ds(mine, uq), :] = mine_sum.astype(BF16)
 
-    across = []
     block = every.at[z, pl.ds(mine, uq)]
-    for k in range(1, n_trade):
-        across.append(send(block, block, every_z_sem, (k,), trade_peer(k)))
-    within = []
-    for k in range(1, n_group):
-        within.append(send(block, block, every_g_sem, (0, k), group_peer(k)))
-    for j in range(1, n_trade):
-        across[j - 1].wait_recv()
-        block = every.at[lax.rem(z + n_trade - j, n_trade), pl.ds(mine, uq)]
-        for k in range(1, n_group):
-            within.append(send(block, block, every_g_sem, (j, k), group_peer(k)))
-    pending += across
-
+    final = [send(block, block, every_sem, (j, k), peer(j, k)) for j, k in others]
     for copy in charges:
         copy.wait_recv()
     pending += charges
@@ -302,9 +334,9 @@
         group_charge = group_charge + charge_far[k]
     charge_ref[...] = group_charge[0:1, :]
 
-    for copy in within:
-        copy.wait_recv()
-    pending += within
+    for copy in final:
+        copy.wait_recv()
+    pending += final
     rows = jnp.zeros((n_u, n_n), F32)
     for o in range(n_trade):
         rows = rows + jnp.dot(every[o], member[o * n_p : (o + 1) * n_p, :], preferred_element_type=F32)
@@ -320,6 +352,17 @@
     flows_ref[...] = lax.fori_loop(0, n_u // 8, pick_step, jnp.zeros((n_k, n_n), F32))
     for copy in pending:
         copy.wait_send()
+
+
+def write_out(charge_ref, flows_ref, charge_out, flows_out, sems):
+    copies = [
+        pltpu.make_async_copy(flows_ref, flows_out, sems.at[0]),
+        pltpu.make_async_copy(charge_ref, charge_out, sems.at[1]),
+    ]
+    for copy in copies:
+        copy.start()
+    for copy in copies:
+        copy.wait()
 
 
 def per_device(
@@ -352,15 +395,25 @@
             jax.ShapeDtypeStruct((1, n_c), F32),
             jax.ShapeDtypeStruct((n_k, n_n), F32),
         ),
-        in_specs=[vmem] * 10 + [pl.BlockSpec(memory_space=pl.ANY)],
+        in_specs=[pl.BlockSpec(memory_space=pltpu.HBM)] * 11,
         out_specs=(vmem, vmem),
         scratch_shapes=[
+            pltpu.VMEM((n_k, n_n), cash_flows.dtype),
+            pltpu.VMEM((n_k, n_n), jnp.int32),
+            pltpu.VMEM((1, n_n), jnp.int32),
+            pltpu.VMEM((1, n_sets), jnp.int32),
+            pltpu.VMEM((1, n_p), jnp.int32),
+            pltpu.VMEM((1, n_p), F32),
+            pltpu.VMEM((1, n_p), jnp.int32),
+            pltpu.VMEM((span, n_c), F32),
+            pltpu.VMEM((1, n_c), F32),
+            pltpu.VMEM((1, n_c), F32),
             pltpu.VMEM((steps, n_u, n_s), BF16),
             pltpu.VMEM((steps, n_s, n_u), BF16),
             pltpu.VMEM((steps, n_s, n_p), F32),
             pltpu.VMEM((steps, n_s, n_p), F32),
-            pltpu.VMEM((steps, n_s, n_p), F32),
-            pltpu.VMEM((steps + LAGMAX, n_s, n_p), F32),
+            pltpu.VMEM((steps, n_s, n_p), BF16),
+            pltpu.VMEM((steps + LAGMAX, n_s, n_p), BF16),
             pltpu.VMEM((span, n_p), F32),
             pltpu.VMEM((span, n_p), F32),
             pltpu.VMEM((n_sets, n_n), BF16),
@@ -376,12 +429,12 @@
             pltpu.VMEM((8, n_c), F32),
             pltpu.VMEM((n_trade, 8, n_c), F32),
             dma,
+            dma((10,)),
             dma((2,)),
             dma((2, n_trade)),
             dma((2, n_group)),
             dma((2, n_group)),
             dma((2, n_group)),
-            dma((2, n_trade)),
             dma((2, n_trade)),
             dma((2, n_trade, n_group)),
         ],
@@ -389,17 +442,22 @@
             collective_id=0, has_side_effects=True, vmem_limit_bytes=48 * 1024 * 1024
         ),
     )(
-        cash_flows.T,
-        coupon_dates.T,
-        trade_sets.reshape(1, -1),
-        set_slots.reshape(1, -1),
-        set_lags.reshape(1, -1),
-        thresholds.reshape(1, -1),
-        set_cpty.reshape(1, -1),
-        default_probs.T,
-        loss_given.reshape(1, -1),
-        cva_cotangent.reshape(1, -1),
-        discounts,
+        *(
+            pltpu.with_memory_space_constraint(a, pltpu.HBM)
+            for a in (
+                cash_flows.T,
+                coupon_dates.T,
+                trade_sets.reshape(1, -1),
+                set_slots.reshape(1, -1),
+                set_lags.reshape(1, -1),
+                thresholds.reshape(1, -1),
+                set_cpty.reshape(1, -1),
+                default_probs.T,
+                loss_given.reshape(1, -1),
+                cva_cotangent.reshape(1, -1),
+                discounts,
+            )
+        )
     )
     return charge.reshape(-1), flow_grads.T
 

time: 45.3 us -> 30.7 us (0.68)
  local copies, waits for them, and re-layouts: 9.71 us -> 1.14 us
  Pallas kernels: 34.5 us -> 28.7 us
    unnamed x24 -> x2, local copies, waits for them, and re-layouts: 9.71 us -> 1.14 us
    pallas_call x1, Pallas kernels: 34.5 us -> 28.7 us  [per_device(): pl.pallas_call(functools.partial(kernel, n_trade, n_date, n_scen), out_sh...]
where the time goes in v2:
time: 30.7 us; the launch traced here: 30.5 us
  Pallas kernels  28.7 us (93%)
  local copies, waits for them, and re-layouts  1.14 us (4%)
  between operations  0.64 us (2%)
    pallas_call x1, Pallas kernels, per_device(): pl.pallas_call(functools.partial(kernel, n_trade, n_date, n_scen), out_sh...  28.7 us
    unnamed x2, local copies, waits for them, and re-layouts  1.14 us

profile of v2, /device:TPU:0, one launch (start us, length us, event | category | flops | bytes accessed | tf_op | source)
XLA Modules:
  0.0 30.5 jit_solution(16461425896124993260)
XLA Ops:
  0.6 28.7 %shard_map.122 = (f32[1,128]{1,0:T(1,128)S(1)}, f32[64,256]{1,0:T(8,128)S(1)}) custom-call(bf16[64,256]{1,0:T(8,128)(2,1)} %bitcast.15, s32[64,256]{1,0:T(8,128)} %bitcast.14, s32[1,256]{1,0:T(1,128)} %bitcast.18, s32[1,512]{1,0:T(1,128)} %bitcast.17, s32[1,128]{1,0:T(1,128)} %bitcast.19, f32[1,128]{1,0:T(1,128)} %bitcast.20, s32[1,128]{1,0:T(1,128)} %bitcast.21, ...), custom_call_target="tpu_custom_call" | custom-call | tf_op jit(solution)/shard_map/pallas_call | solution.py:392
  29.4 0.5 %copy.15 = f32[128]{0:T(128)} copy(f32[128]{0:T(128)S(1)} %bitcast.13) | data formatting | bytes 1024
  29.9 0.6 %copy.16 = f32[256,64]{0,1:T(8,128)} copy(f32[256,64]{0,1:T(8,128)S(1)} %bitcast.12) | data formatting | bytes 131072

commit v3 on v2

--- a/solution.py
+++ b/solution.py
@@ -9,16 +9,13 @@
 
 LAGMAX = 4
 RATE = 10.0
+SLAB = 32
+LOG2 = 0.6931471805599453
 STEP = 4
 MESH = pl.DeviceIdType.MESH
 NT = (((1,), (1,)), ((), ()))
 F32 = jnp.float32
 BF16 = jnp.bfloat16
-
-
-def smooth(a):
-    g = 0.5 + 0.5 * jnp.tanh(0.5 * a)
-    return jnp.maximum(a, 0.0) - jnp.log(jnp.maximum(g, 1.0 - g)), g
 
 
 def exact_dot(a, b, dims=(((1,), (0,)), ((), ()))):
@@ -61,9 +58,9 @@
     hazard,
     weight,
     member,
+    parts,
     parts_out,
     parts_in,
-    set_flows,
     total,
     total_in,
     every,
@@ -76,7 +73,6 @@
     small_sem,
     halo_sem,
     parts_sem,
-    flow_sem,
     total_sem,
     charge_sem,
     far_sem,
@@ -105,6 +101,8 @@
         return {"date": peer // n_scen, "scen": lax.rem(peer, n_scen)}
 
     others = [(j, k) for j in range(n_trade) for k in range(n_group) if j + k > 0]
+
+    near = [(j, k) for j, k in others if j * k == 0]
 
     def peer(j, k):
         return {**trade_peer(j), **group_peer(k)}
@@ -151,8 +149,8 @@
         copy.wait()
 
     mine = pl.multiple_of(g * uq, uq)
-    u_rows = lax.broadcasted_iota(jnp.int32, (uq, n_n), 0) + g * uq
-    grid = jnp.zeros((uq, n_n), F32)
+    u_rows = lax.broadcasted_iota(jnp.int32, (n_u, n_n), 0)
+    grid = jnp.zeros((n_u, n_n), F32)
     cash = cash_ref[...].astype(F32)
     moments = dates_ref[...]
     for k in range(n_k):
@@ -168,7 +166,9 @@
     member[...] = (p_rows == positions).astype(F32).astype(BF16)
     partial = lax.dot_general(grid.astype(BF16), member[...], NT, preferred_element_type=F32)
     for o in range(n_trade):
-        parts_out[o] = partial[:, o * n_p : (o + 1) * n_p]
+        own_part = partial[:, o * n_p : (o + 1) * n_p]
+        parts[o] = own_part
+        parts_out[o] = own_part.astype(BF16)
 
     pl.semaphore_wait(barrier, len(others))
     pending = []
@@ -189,7 +189,7 @@
     scales = exact_dot(scales, named)
     paths = float(n_s * n_scen)
     hazard[...] = exact_dot(probs_ref[...], named)
-    weight[...] = hazard[...] * (scales[1:2, :] / paths)
+    weight[...] = hazard[...] * (scales[1:2, :] * (0.5 / paths))
 
     u_col = lax.broadcasted_iota(jnp.int32, (n_u, n_s), 0)
 
@@ -211,25 +211,16 @@
     for copy in arrivals:
         copy.wait_recv()
     pending += arrivals
-    mine_sum = parts_out[z]
+    flow_sum = parts[z]
     for k in range(1, n_trade):
-        mine_sum = mine_sum + parts_in[k]
-    set_flows[pl.ds(mine, uq), :] = mine_sum.astype(BF16)
-    arrivals = []
-    for k in range(1, n_group):
-        block = set_flows.at[pl.ds(mine, uq)]
-        arrivals.append(send(block, block, flow_sem, (k,), group_peer(k)))
+        flow_sum = flow_sum + parts_in[k].astype(F32)
+    flows = flow_sum.astype(BF16)
 
     halo.wait()
     after_first = jnp.where(d > 0, 1.0, 0.0).astype(F32)
     for b in range(LAGMAX):
         mask_dates(b, after_first)
-    for copy in arrivals:
-        copy.wait_recv()
-    pending += arrivals
-
-    flows = set_flows[...]
-    limits = limits_ref[...] * RATE
+    limits = limits_ref[...] * (0.5 * RATE)
 
     lags = lags_ref[...]
     lags16 = lags.astype(F32).astype(BF16)
@@ -241,35 +232,54 @@
         return out
 
     def value_block(i, shown=None):
-        for b in range(LAGMAX):
-            t = i * LAGMAX + b
-            v = jnp.dot(fwd_t[t], flows, preferred_element_type=F32) * RATE
-            amount, slope = smooth(v - limits)
-            if shown is not None:
-                amount, slope = amount * shown, slope * shown
-            vals[t] = v
-            coll[t] = amount
-            gate[t] = slope.astype(BF16)
+        base = pl.multiple_of(i * LAGMAX, LAGMAX)
+        rows = fwd_t[pl.ds(base, LAGMAX)].reshape(LAGMAX * n_s, n_u)
+        v = jnp.dot(rows, flows, preferred_element_type=F32) * (0.5 * RATE)
+        a = v - limits
+        half = 0.5 * jnp.tanh(a)
+        amount = jnp.maximum(a, 0.0) - 0.5 * jnp.log(0.5 + jnp.abs(half))
+        slope = 0.5 + half
+        if shown is not None:
+            amount, slope = amount * shown, slope * shown
+        shape = (LAGMAX, n_s, n_p)
+        vals[pl.ds(base, LAGMAX)] = v.reshape(shape)
+        coll[pl.ds(base, LAGMAX)] = amount.reshape(shape)
+        gate[pl.ds(base, LAGMAX)] = slope.astype(BF16).reshape(shape)
 
     def exposure_block(i, acc):
         for b in range(LAGMAX):
             t = i * LAGMAX + b
-            margin = vals[t] - by_lag(lags, [coll[t - lag] for lag in range(LAGMAX + 1)])
-            amount, slope = smooth(margin)
             own = pl.ds(t - LAGMAX, 1)
-            acc = acc + jnp.sum(amount.reshape(-1, 8, n_p), axis=0) * hazard[own, :]
-            direct[t] = (slope * weight[own, :]).astype(BF16)
+            scale = weight[own, :]
+            gain = jnp.zeros((8, n_p), F32)
+            for low in range(0, n_s, SLAB):
+                at = pl.ds(low, SLAB)
+                margin = vals[t, at] - by_lag(lags, [coll[t - lag, at] for lag in range(LAGMAX + 1)])
+                turn = jnp.tanh(margin)
+                direct[t, at] = (scale + scale * turn).astype(BF16)
+                factors = 1.0 + jnp.abs(turn)
+                product = factors[0:8]
+                for m in range(8, SLAB, 8):
+                    product = product * factors[m : m + 8]
+                above = jnp.sum(jnp.maximum(margin, 0.0).reshape(SLAB // 8, 8, n_p), axis=0)
+                gain = gain + (above - 0.5 * jnp.log(product))
+            acc = acc + (gain + 0.5 * LOG2 * (n_s // 8)) * hazard[own, :]
         return acc
 
     def grad_block(i):
-        out = None
+        blocks, rows = [], []
         for b in range(LAGMAX):
             t = i * LAGMAX + b
-            later = by_lag(lags16, [direct[t + lag] for lag in range(LAGMAX + 1)])
-            block = direct[t] - later * gate[t]
-            term = jnp.dot(fwd[t], block, preferred_element_type=F32)
-            out = term if out is None else out + term
-        total[...] += out
+            for low in range(0, n_s, SLAB):
+                at = pl.ds(low, SLAB)
+                later = by_lag(lags16, [direct[t + lag, at] for lag in range(LAGMAX + 1)])
+                blocks.append(direct[t, at] - later * gate[t, at])
+            rows.append(fwd[t])
+        total[...] += jnp.dot(
+            jnp.concatenate(rows, axis=1),
+            jnp.concatenate(blocks, axis=0),
+            preferred_element_type=F32,
+        )
 
     for b in range(LAGMAX):
         direct[b] = jnp.zeros((n_s, n_p), BF16)
@@ -290,7 +300,7 @@
 
     acc = lax.fori_loop(3, last + 1, block_step, acc)
     acc = exposure_block(last, acc)
-    terms = jnp.sum(acc, axis=0, keepdims=True) * (scales[0:1, :] * (1.0 / (RATE * paths)))
+    terms = jnp.sum(acc, axis=0, keepdims=True) * (scales[0:1, :] * (2.0 / (RATE * paths)))
     charge_out[...] = exact_dot(jnp.broadcast_to(terms, (8, n_p)), named, NT)
     charges = []
     for k in range(1, n_group):
@@ -325,7 +335,7 @@
     every[z, pl.ds(mine, uq), :] = mine_sum.astype(BF16)
 
     block = every.at[z, pl.ds(mine, uq)]
-    final = [send(block, block, every_sem, (j, k), peer(j, k)) for j, k in others]
+    final = [send(block, block, every_sem, (j, k), peer(j, k)) for j, k in sorted(others, key=lambda p: (p[0], -p[1]))]
     for copy in charges:
         copy.wait_recv()
     pending += charges
@@ -417,9 +427,9 @@
             pltpu.VMEM((span, n_p), F32),
             pltpu.VMEM((span, n_p), F32),
             pltpu.VMEM((n_sets, n_n), BF16),
-            pltpu.VMEM((n_trade, uq, n_p), F32),
-            pltpu.VMEM((n_trade, uq, n_p), F32),
-            pltpu.VMEM((n_u, n_p), BF16),
+            pltpu.VMEM((n_trade, n_u, n_p), F32),
+            pltpu.VMEM((n_trade, n_u, n_p), BF16),
+            pltpu.VMEM((n_trade, n_u, n_p), BF16),
             pltpu.VMEM((n_u, n_p), F32),
             pltpu.VMEM((n_group, uq, n_p), F32),
             pltpu.VMEM((n_trade, n_u, n_p), BF16),
@@ -432,7 +442,6 @@
             dma((10,)),
             dma((2,)),
             dma((2, n_trade)),
-            dma((2, n_group)),
             dma((2, n_group)),
             dma((2, n_group)),
             dma((2, n_trade)),

time: 30.7 us -> 28.6 us (0.932)
  Pallas kernels: 28.7 us -> 26.7 us
    pallas_call x1, Pallas kernels: 28.7 us -> 26.7 us  [per_device(): pl.pallas_call(functools.partial(kernel, n_trade, n_date, n_scen), out_sh...]
where the time goes in v3:
time: 28.6 us; the launch traced here: 28.4 us
  Pallas kernels  26.7 us (93%)
  local copies, waits for them, and re-layouts  1.14 us (4%)
  between operations  0.64 us (2%)
    pallas_call x1, Pallas kernels, per_device(): pl.pallas_call(functools.partial(kernel, n_trade, n_date, n_scen), out_sh...  26.7 us
    unnamed x2, local copies, waits for them, and re-layouts  1.14 us

profile of v3, /device:TPU:0, one launch (start us, length us, event | category | flops | bytes accessed | tf_op | source)
XLA Modules:
  0.0 28.4 jit_solution(8470734405564827618)
XLA Ops:
  0.6 26.7 %shard_map.122 = (f32[1,128]{1,0:T(1,128)S(1)}, f32[64,256]{1,0:T(8,128)S(1)}) custom-call(bf16[64,256]{1,0:T(8,128)(2,1)} %bitcast.15, s32[64,256]{1,0:T(8,128)} %bitcast.14, s32[1,256]{1,0:T(1,128)} %bitcast.18, s32[1,512]{1,0:T(1,128)} %bitcast.17, s32[1,128]{1,0:T(1,128)} %bitcast.19, f32[1,128]{1,0:T(1,128)} %bitcast.20, s32[1,128]{1,0:T(1,128)} %bitcast.21, ...), custom_call_target="tpu_custom_call" | custom-call | tf_op jit(solution)/shard_map/pallas_call | solution.py:402
  27.3 0.5 %copy.15 = f32[128]{0:T(128)} copy(f32[128]{0:T(128)S(1)} %bitcast.13) | data formatting | bytes 1024
  27.8 0.6 %copy.16 = f32[256,64]{0,1:T(8,128)} copy(f32[256,64]{0,1:T(8,128)S(1)} %bitcast.12) | data formatting | bytes 131072

commit v4 on v3

--- a/solution.py
+++ b/solution.py
@@ -58,9 +58,9 @@
     hazard,
     weight,
     member,
-    parts,
     parts_out,
     parts_in,
+    set_flows,
     total,
     total_in,
     every,
@@ -73,6 +73,7 @@
     small_sem,
     halo_sem,
     parts_sem,
+    flow_sem,
     total_sem,
     charge_sem,
     far_sem,
@@ -149,8 +150,8 @@
         copy.wait()
 
     mine = pl.multiple_of(g * uq, uq)
-    u_rows = lax.broadcasted_iota(jnp.int32, (n_u, n_n), 0)
-    grid = jnp.zeros((n_u, n_n), F32)
+    u_rows = lax.broadcasted_iota(jnp.int32, (uq, n_n), 0) + g * uq
+    grid = jnp.zeros((uq, n_n), F32)
     cash = cash_ref[...].astype(F32)
     moments = dates_ref[...]
     for k in range(n_k):
@@ -166,9 +167,7 @@
     member[...] = (p_rows == positions).astype(F32).astype(BF16)
     partial = lax.dot_general(grid.astype(BF16), member[...], NT, preferred_element_type=F32)
     for o in range(n_trade):
-        own_part = partial[:, o * n_p : (o + 1) * n_p]
-        parts[o] = own_part
-        parts_out[o] = own_part.astype(BF16)
+        parts_out[o] = partial[:, o * n_p : (o + 1) * n_p]
 
     pl.semaphore_wait(barrier, len(others))
     pending = []
@@ -211,15 +210,24 @@
     for copy in arrivals:
         copy.wait_recv()
     pending += arrivals
-    flow_sum = parts[z]
+    mine_sum = parts_out[z]
     for k in range(1, n_trade):
-        flow_sum = flow_sum + parts_in[k].astype(F32)
-    flows = flow_sum.astype(BF16)
+        mine_sum = mine_sum + parts_in[k]
+    set_flows[pl.ds(mine, uq), :] = mine_sum.astype(BF16)
+    arrivals = []
+    for k in range(1, n_group):
+        block = set_flows.at[pl.ds(mine, uq)]
+        arrivals.append(send(block, block, flow_sem, (k,), group_peer(k)))
 
     halo.wait()
     after_first = jnp.where(d > 0, 1.0, 0.0).astype(F32)
     for b in range(LAGMAX):
         mask_dates(b, after_first)
+    for copy in arrivals:
+        copy.wait_recv()
+    pending += arrivals
+
+    flows = set_flows[...]
     limits = limits_ref[...] * (0.5 * RATE)
 
     lags = lags_ref[...]
@@ -427,9 +435,9 @@
             pltpu.VMEM((span, n_p), F32),
             pltpu.VMEM((span, n_p), F32),
             pltpu.VMEM((n_sets, n_n), BF16),
-            pltpu.VMEM((n_trade, n_u, n_p), F32),
-            pltpu.VMEM((n_trade, n_u, n_p), BF16),
-            pltpu.VMEM((n_trade, n_u, n_p), BF16),
+            pltpu.VMEM((n_trade, uq, n_p), F32),
+            pltpu.VMEM((n_trade, uq, n_p), F32),
+            pltpu.VMEM((n_u, n_p), BF16),
             pltpu.VMEM((n_u, n_p), F32),
             pltpu.VMEM((n_group, uq, n_p), F32),
             pltpu.VMEM((n_trade, n_u, n_p), BF16),
@@ -442,6 +450,7 @@
             dma((10,)),
             dma((2,)),
             dma((2, n_trade)),
+            dma((2, n_group)),
             dma((2, n_group)),
             dma((2, n_group)),
             dma((2, n_trade)),

time: 28.6 us -> 30.2 us (1.056)
  Pallas kernels: 26.7 us -> 28.3 us
    pallas_call x1, Pallas kernels: 26.7 us -> 28.3 us  [per_device(): pl.pallas_call(functools.partial(kernel, n_trade, n_date, n_scen), out_sh...]
where the time goes in v4:
time: 30.2 us; the launch traced here: 30.1 us
  Pallas kernels  28.3 us (94%)
  local copies, waits for them, and re-layouts  1.14 us (4%)
  between operations  0.64 us (2%)
    pallas_call x1, Pallas kernels, per_device(): pl.pallas_call(functools.partial(kernel, n_trade, n_date, n_scen), out_sh...  28.3 us
    unnamed x2, local copies, waits for them, and re-layouts  1.14 us

profile of v4, /device:TPU:0, one launch (start us, length us, event | category | flops | bytes accessed | tf_op | source)
XLA Modules:
  0.0 30.1 jit_solution(14164263536456054770)
XLA Ops:
  0.6 28.3 %shard_map.122 = (f32[1,128]{1,0:T(1,128)S(1)}, f32[64,256]{1,0:T(8,128)S(1)}) custom-call(bf16[64,256]{1,0:T(8,128)(2,1)} %bitcast.15, s32[64,256]{1,0:T(8,128)} %bitcast.14, s32[1,256]{1,0:T(1,128)} %bitcast.18, s32[1,512]{1,0:T(1,128)} %bitcast.17, s32[1,128]{1,0:T(1,128)} %bitcast.19, f32[1,128]{1,0:T(1,128)} %bitcast.20, s32[1,128]{1,0:T(1,128)} %bitcast.21, ...), custom_call_target="tpu_custom_call" | custom-call | tf_op jit(solution)/shard_map/pallas_call | solution.py:410
  28.9 0.5 %copy.15 = f32[128]{0:T(128)} copy(f32[128]{0:T(128)S(1)} %bitcast.13) | data formatting | bytes 1024
  29.4 0.6 %copy.16 = f32[256,64]{0,1:T(8,128)} copy(f32[256,64]{0,1:T(8,128)S(1)} %bitcast.12) | data formatting | bytes 131072
